TPU v7x, 32 devices: a whole 2x2x4 slice. The times are simulated.
32 devices in a mesh: section: 2 (over x), dp: 4 (over y, core), tensor: 4 (over z).
Axes of the slice: x: 2, y: 2, z: 4, core: 2. Of those that a mesh axis runs over, the one named last changes fastest.
Arguments:
- tokens_in: bfloat16 [2, 7168, 1024], P(None, 'tensor', 'dp'), may hold values from -47 to 47
- section_proj: bfloat16 [2, 7168, 7168], P('section', 'tensor'), may hold values from -0.0625 to 0.0625
- section_gain: bfloat16 [2, 7168], P('section', 'tensor'), may hold values from 0.099609375 to 1.8984375
- final_gain: bfloat16 [7168], P('tensor'), may hold values from 0.099609375 to 1.8984375
- score_weight: bfloat16 [7168], P('tensor'), may hold values from -0.0625 to 0.0625
- labels: int32 [2, 1024], P(None, 'dp'), may hold values from 0 to 2
- loss_mask: int32 [2, 1024], P(None, 'dp'), may hold values 0 or 1
- segment_ids: int32 [2, 1024], P(None, 'dp'), may hold values from 0 to 15, never falling along the last dimension, each value on 1 to 512 neighbouring positions
Outputs:
- section_out: bfloat16 [2, 2, 7168, 1024], P('section', None, 'tensor', 'dp')
- segment_loss: float32 [2, 16], replicated
Inputs may be any that keep to these rules, and one draw needn't show every extreme that they name: `segment_ids`: within a micro-batch segment numbers never fall along the tokens; each segment has 1 to 512 tokens.
All inputs are finite; a program needn't handle non-finite values. No bound on the sum of `loss_mask` on one device may be relied on, other than what follows from the above.
Results may differ from a plain program's by a relative error of at most 0.0045.
Values may be sent and summed in bfloat16 or wider, within the bound.
A program may use at most 64 MiB of HBM per device.

v0:
```python
import jax
import jax.numpy as jnp
from jax import lax
from jax.sharding import PartitionSpec as P

D = 7168
SEGS = 16


epsilon = 1e-05


def passed_along(shard, axis, by):
    count = lax.axis_size(axis)
    pairs = [(i, i + by) for i in range(count) if 0 <= i + by < count]
    return lax.ppermute(shard, axis, pairs)


def body(
    tokens_in, section_proj, section_gain, final_gain, score_weight, labels, loss_mask, segment_ids
):
    section_index = lax.axis_index("section")
    weight_local = section_proj[0]
    gain_local = section_gain[0]
    head_vector = final_gain.astype(jnp.float32) * score_weight.astype(jnp.float32)
    micro_count = tokens_in.shape[0]
    received = jnp.zeros_like(tokens_in[0])
    produced = []
    score_list = []
    for moment in range(micro_count + 1):
        if moment < micro_count:
            fresh_rows = tokens_in[moment]
        else:
            fresh_rows = jnp.zeros_like(tokens_in[0])
        incoming = jnp.where(section_index == 0, fresh_rows, received)
        apply_as_float = incoming.astype(jnp.float32)
        apply_squares = lax.psum(jnp.sum(apply_as_float * apply_as_float, axis=0), "tensor")
        apply_inv_root = lax.rsqrt(apply_squares / D + epsilon)[None, :]
        normed = (apply_as_float * apply_inv_root * gain_local.astype(jnp.float32)[:, None]).astype(
            jnp.bfloat16
        )
        mixed = jnp.dot(
            weight_local,
            lax.all_gather(normed, "tensor", axis=0, tiled=True),
            preferred_element_type=jnp.float32,
        )
        result_rows = (apply_as_float + jax.nn.silu(mixed)).astype(jnp.bfloat16)
        produced.append(result_rows)
        if moment < micro_count:
            received = passed_along(result_rows, "section", 1)
        if moment >= 1:
            as_float = result_rows.astype(jnp.float32)
            squares_part = jnp.sum(as_float * as_float, axis=0)
            squares = lax.psum(squares_part, "tensor")
            inv_root = lax.rsqrt(squares / D + epsilon)
            partial_score = jnp.sum(as_float * inv_root[None, :] * head_vector[:, None], axis=0)
            score_list.append(lax.psum(partial_score, "tensor"))
    section_out = jnp.where(
        section_index == 0, jnp.stack(produced[:micro_count]), jnp.stack(produced[1:])
    )[None]
    segment_range = lax.broadcasted_iota(jnp.int32, (1, SEGS), 1)
    sum_rows = []
    count_rows = []
    for micro in range(micro_count):
        target = labels[micro].astype(jnp.float32) - 1.0
        weight_mask = loss_mask[micro].astype(jnp.float32)
        offset_err = score_list[micro] - target
        squared = weight_mask * offset_err * offset_err
        member = (segment_ids[micro][:, None] == segment_range).astype(jnp.float32)
        sum_rows.append(jnp.dot(squared, member, precision=lax.Precision.HIGHEST))
        count_rows.append(jnp.dot(weight_mask, member, precision=lax.Precision.HIGHEST))
    live_section = (section_index == 1).astype(jnp.float32)
    loss_sums, counted = lax.psum(
        (jnp.stack(sum_rows) * live_section, jnp.stack(count_rows) * live_section),
        ("section", "dp"),
    )
    segment_loss = loss_sums / jnp.maximum(counted, 1.0)
    return (section_out, segment_loss)


def solution(mesh):
    in_specs = (
        P(None, "tensor", "dp"),
        P("section", "tensor", None),
        P("section", "tensor"),
        P("tensor"),
        P("tensor"),
        P(None, "dp"),
        P(None, "dp"),
        P(None, "dp"),
    )
    out_specs = (P("section", None, "tensor", "dp"), P())
    return jax.shard_map(body, mesh=mesh, in_specs=in_specs, out_specs=out_specs, check_vma=False)
```

profile of v0, /device:TPU:0, one launch (start us, length us, event | category | flops | bytes accessed | tf_op | source)
XLA Modules:
  0.0 394.5 jit_solution(9843444816501216504)
XLA Ops:
  7.2 0.0 all-gather.4.cloned.1.call-start
  7.2 1.6 fusion.49
  8.8 0.0 copy-start.1
  8.8 0.6 copy.13
  9.4 0.3 fusion.29
  9.8 13.5 %psum.63 = f32[256]{0:T(256)S(1)} all-reduce(f32[256]{0:T(256)S(1)} %fusion.29), channel_id=1, replica_groups=mesh['section'=2,'dp'=4,'tensor'=4] {'tensor'}, use_global_device_ids=true, to_apply=%region_1.2 | all-reduce | flops 256 | bytes 2048 | tf_op jit(solution)/shard_map/psum | solution.py:37
  23.2 0.0 copy-done.1
  23.3 1.2 fusion.31
  24.5 0.0 all-gather.4.cloned.1.call-update
  24.5 0.0 all-gather.6.cloned.1.call-start
  24.5 70.4 %all-gather.4.cloned.1.call-done = bf16[7168,256]{0,1:T(8,128)(2,1)} async-done(((bf16[1792,256]{0,1:T(8,128)(2,1)}), bf16[7168,256]{0,1:T(8,128)(2,1)}) %all-gather.4.cloned.1.call-update) | async-done | bytes 3670032 | tf_op jit(solution)/shard_map/all_gather | solution.py:44
  95.0 14.7 %fusion.32 = bf16[1792,256]{0,1:T(8,128)(2,1)} fusion(bf16[7168,256]{0,1:T(8,128)(2,1)} %all-gather.4.cloned.1.call-done, bf16[1,1792,7168]{2,1,0:T(8,128)(2,1)} %param.9, bf16[1,1792,256]{1,2,0:T(8,128)(2,1)S(1)} %copy.13, pred[]{:T(512)S(6)} %eq.39), kind=kOutput, calls=%fused_computation.39 | convolution fusion | flops 6580338688 | bytes 31195136 | tf_op jit(solution)/shard_map/dot_general | solution.py:42
  109.7 4.3 %collective-permute-start = (bf16[1792,256]{0,1:T(8,128)(2,1)}, bf16[1792,256]{0,1:T(8,128)(2,1)}, u32[]{:S(2)}, u32[]{:S(2)}) collective-permute-start(bf16[1792,256]{0,1:T(8,128)(2,1)} %fusion.32), channel_id=1, source_target_pairs={{0,16},{1,17},{2,18},{3,19},{4,20},{5,21},{6,22},{7,23},{8,24},{9,... | collective-permute-start | bytes 2752520 | tf_op jit(solution)/shard_map/ppermute | solution.py:16
  114.0 0.6 copy.14
  114.6 18.4 %collective-permute-done = bf16[1792,256]{0,1:T(8,128)(2,1)} collective-permute-done((bf16[1792,256]{0,1:T(8,128)(2,1)}, bf16[1792,256]{0,1:T(8,128)(2,1)}, u32[]{:S(2)}, u32[]{:S(2)}) %collective-permute-start) | collective-permute-done | bytes 917536 | tf_op jit(solution)/shard_map/ppermute | solution.py:16
  133.0 0.4 fusion.21
  133.4 9.5 %psum.64 = f32[256]{0:T(256)S(1)} all-reduce(f32[256]{0:T(256)S(1)} %get-tuple-element.12), channel_id=1, replica_groups=mesh['section'=2,'dp'=4,'tensor'=4] {'tensor'}, use_global_device_ids=true, to_apply=%region_3.4 | all-reduce | flops 256 | bytes 2048 | tf_op jit(solution)/shard_map/psum | solution.py:37
  142.9 1.2 fusion.23
  144.1 0.0 all-gather.6.cloned.1.call-update
  144.1 0.0 all-gather.8.cloned.1.call-start
  144.1 72.9 %all-gather.6.cloned.1.call-done = bf16[7168,256]{0,1:T(8,128)(2,1)} async-done(((bf16[1792,256]{0,1:T(8,128)(2,1)}), bf16[7168,256]{0,1:T(8,128)(2,1)}) %all-gather.6.cloned.1.call-update) | async-done | bytes 3670032 | tf_op jit(solution)/shard_map/all_gather | solution.py:44
  217.0 14.1 %fusion.15 = (f32[256]{0:T(256)S(1)}, bf16[1792,256]{0,1:T(8,128)(2,1)S(1)}) fusion(bf16[7168,256]{0,1:T(8,128)(2,1)} %all-gather.6.cloned.1.call-done, bf16[1,1792,7168]{2,1,0:T(8,128)(2,1)} %param.9, bf16[1792,256]{0,1:T(8,128)(2,1)S(1)} %get-tuple-element.13), kind=kOutput, calls=%fused_computation.22 | convolution fusion | flops 6581256192 | bytes 31196160 | tf_op jit(solution)/shard_map/dot_general | solution.py:42
  231.2 0.0 copy-start.4
  231.2 0.0 copy-start.5
  231.2 0.0 copy-start.6
  231.2 0.0 copy-start.2
  231.2 0.0 copy-start.3
  231.2 3.6 collective-permute-start.1
  234.8 19.5 %collective-permute-done.1 = bf16[1792,256]{0,1:T(8,128)(2,1)S(1)} collective-permute-done((bf16[1792,256]{0,1:T(8,128)(2,1)S(1)}, bf16[1792,256]{0,1:T(8,128)(2,1)S(1)}, u32[]{:S(2)}, u32[]{:S(2)}) %collective-permute-start.1) | collective-permute-done | bytes 917536 | tf_op jit(solution)/shard_map/ppermute | solution.py:16
  254.4 0.3 fusion.25
  254.7 9.7 %psum.65 = f32[256]{0:T(256)S(1)} all-reduce(f32[256]{0:T(256)S(1)} %fusion.25), channel_id=1, replica_groups=mesh['section'=2,'dp'=4,'tensor'=4] {'tensor'}, use_global_device_ids=true, to_apply=%region_5.6 | all-reduce | flops 256 | bytes 2048 | tf_op jit(solution)/shard_map/psum | solution.py:37
  264.4 1.2 fusion.27
  265.6 0.0 all-gather.8.cloned.1.call-update
  265.6 0.0 copy-done.4
  265.6 0.0 copy-done.5
  265.6 0.2 fusion.39
  265.9 0.2 fusion.41
  266.1 0.0 copy-done.6
  266.2 0.0 copy-done.2
  266.2 0.0 copy-done.3
  266.2 71.2 %all-gather.8.cloned.1.call-done = bf16[7168,256]{0,1:T(8,128)(2,1)} async-done(((bf16[1792,256]{0,1:T(8,128)(2,1)}), bf16[7168,256]{0,1:T(8,128)(2,1)}) %all-gather.8.cloned.1.call-update) | async-done | bytes 3670032 | tf_op jit(solution)/shard_map/all_gather | solution.py:44
  337.4 14.2 %fusion.18 = (f32[256]{0:T(256)S(1)}, bf16[1792,256]{0,1:T(8,128)(2,1)S(1)}) fusion(bf16[7168,256]{0,1:T(8,128)(2,1)} %all-gather.8.cloned.1.call-done, bf16[1,1792,7168]{2,1,0:T(8,128)(2,1)} %param.9, bf16[1792,256]{0,1:T(8,128)(2,1)S(1)} %collective-permute-done.1, pred[]{:T(512)S(6)} %eq.39), kind=kOutput, calls=%fused_computation.25 | convolution fusion | flops 6581714944 | bytes 31196160 | tf_op jit(solution)/shard_map/dot_general | solution.py:42
  351.6 0.0 copy-start
  351.6 9.0 %all-reduce.2 = (f32[256]{0:T(256)S(1)}, f32[256]{0:T(256)S(1)}) all-reduce(f32[256]{0:T(256)S(1)} %get-tuple-element.22, f32[256]{0:T(256)S(1)} %get-tuple-element.24), channel_id=1, replica_groups=mesh['section'=2,'dp'=4,'tensor'=4] {'tensor'}, use_global_device_ids=true, to_apply=%region_7.8 | all-reduce | flops 512 | bytes 4096 | tf_op jit(solution)/shard_map/psum | solution.py:54
  360.6 0.6 fusion.17
  361.2 9.7 %all-reduce.1 = (f32[256]{0:T(256)S(1)}, f32[256]{0:T(256)S(1)}) all-reduce(f32[256]{0:T(256)S(1)} %get-tuple-element.5, f32[256]{0:T(256)S(1)} %get-tuple-element.4), channel_id=1, replica_groups=mesh['section'=2,'dp'=4,'tensor'=4] {'tensor'}, use_global_device_ids=true, to_apply=%region_13.14 | all-reduce | flops 512 | bytes 4096 | tf_op jit(solution)/shard_map/psum | solution.py:57
  371.0 0.2 fusion.42
  371.2 0.2 fusion.40
  371.4 0.0 copy-done
  371.4 1.8 maximum_select_fusion
  373.2 2.3 copy.12
  375.5 11.8 %all-reduce = (f32[2,16]{1,0:T(2,128)S(1)}, f32[2,16]{1,0:T(2,128)S(1)}) all-reduce(f32[2,16]{1,0:T(2,128)S(1)} %maximum_multiply_fusion, f32[2,16]{1,0:T(2,128)S(1)} %maximum_multiply_fusion.1), channel_id=1, replica_groups=mesh['section'=2,'dp'=4,'tensor'=4] {'section','dp'}, use_global_device_ids=true, to_apply=%region_14.15 | all-reduce | flops 64 | bytes 512 | tf_op jit(solution)/shard_map/psum | solution.py:73
  387.4 0.6 maximum_divide_fusion
  (13 shorter events, 0.1 us)
Async XLA Ops:
  7.2 87.8 %all-gather.4.cloned.1.call-start = ((), (), s32[]{:S(2)}) async-start(), calls=%async_computation | async-start | bytes 4587520 | tf_op jit(solution)/shard_map/all_gather | solution.py:44
  8.8 14.4 %copy-start.1 = (bf16[1,1792]{1,0:T(2,128)(2,1)S(1)}, bf16[1,1792]{1,0:T(2,128)(2,1)}, u32[]{:S(2)}) copy-start(bf16[1,1792]{1,0:T(2,128)(2,1)} %param.10) | copy-start | bytes 10756
  24.5 192.5 %all-gather.6.cloned.1.call-start = ((), (), s32[]{:S(2)}) async-start(), calls=%async_computation.1 | async-start | bytes 4587520 | tf_op jit(solution)/shard_map/all_gather | solution.py:44
  109.7 23.3 %collective-permute-start = (bf16[1792,256]{0,1:T(8,128)(2,1)}, bf16[1792,256]{0,1:T(8,128)(2,1)}, u32[]{:S(2)}, u32[]{:S(2)}) collective-permute-start(bf16[1792,256]{0,1:T(8,128)(2,1)} %fusion.32), channel_id=1, source_target_pairs={{0,16},{1,17},{2,18},{3,19},{4,20},{5,21},{6,22},{7,23},{8,24},{9,... | collective-permute-start | bytes 2752520 | tf_op jit(solution)/shard_map/ppermute | solution.py:16
  144.1 193.3 %all-gather.8.cloned.1.call-start = ((), (), s32[]{:S(2)}) async-start(), calls=%async_computation.2 | async-start | bytes 4587520 | tf_op jit(solution)/shard_map/all_gather | solution.py:44
  231.2 34.4 %copy-start.4 = (s32[2,256]{1,0:T(2,128)S(1)}, s32[2,256]{1,0:T(2,128)}, u32[]{:S(2)}) copy-start(s32[2,256]{1,0:T(2,128)} %param.15) | copy-start | bytes 6148
  231.2 34.4 %copy-start.5 = (s32[2,256]{1,0:T(2,128)S(1)}, s32[2,256]{1,0:T(2,128)}, u32[]{:S(2)}) copy-start(s32[2,256]{1,0:T(2,128)} %param.14) | copy-start | bytes 6148
  231.2 34.9 %copy-start.6 = (s32[2,256]{1,0:T(2,128)S(1)}, s32[2,256]{1,0:T(2,128)}, u32[]{:S(2)}) copy-start(s32[2,256]{1,0:T(2,128)} %param.13) | copy-start | bytes 6148
  231.2 34.9 %copy-start.2 = (bf16[1792]{0:T(1024)(128)(2,1)S(1)}, bf16[1792]{0:T(1024)(128)(2,1)}, u32[]{:S(2)}) copy-start(bf16[1792]{0:T(1024)(128)(2,1)} %param.12) | copy-start | bytes 10756
  231.2 34.9 %copy-start.3 = (bf16[1792]{0:T(1024)(128)(2,1)S(1)}, bf16[1792]{0:T(1024)(128)(2,1)}, u32[]{:S(2)}) copy-start(bf16[1792]{0:T(1024)(128)(2,1)} %param.11) | copy-start | bytes 10756
  231.2 23.1 %collective-permute-start.1 = (bf16[1792,256]{0,1:T(8,128)(2,1)S(1)}, bf16[1792,256]{0,1:T(8,128)(2,1)S(1)}, u32[]{:S(2)}, u32[]{:S(2)}) collective-permute-start(bf16[1792,256]{0,1:T(8,128)(2,1)S(1)} %get-tuple-element.23), channel_id=1, source_target_pairs={{0,16},{1,17},{2,18},{3,19},{4,20},{5,21},{6,22},{7,23},{8,24},{9,... | collective-permute-start | bytes 2752520 | tf_op jit(solution)/shard_map/ppermute | solution.py:16
  351.6 19.9 %copy-start = (bf16[1792,256]{0,1:T(8,128)(2,1)}, bf16[1792,256]{0,1:T(8,128)(2,1)S(1)}, u32[]{:S(2)}) copy-start(bf16[1792,256]{0,1:T(8,128)(2,1)S(1)} %get-tuple-element.25) | copy-start | bytes 2752516
Sparse Core Ops, SparseCore 0:
  24.6 70.3 all-gather.3
  144.2 72.7 all-gather.5
  265.7 71.5 all-gather.7
where the time goes:
time: 395 us; the launch traced here: 394 us
  waiting for transfers between devices  252 us (64%)
  blocking collectives  63.2 us (16%)
  matrix products  44 us (11%)
  between operations  14 us (4%)
  starting transfers between devices  7.99 us (2%)
  other arithmetic  7.74 us (2%)
  local copies, waits for them, and re-layouts  5.16 us (1%)
    all_gather x3, waiting for transfers between devices, body(): lax.all_gather(normed, 'tensor', axis=0, tiled=True)  214 us
    dot_general x3, matrix products, body(): jnp.dot(weight_local, lax.all_gather(normed, 'tensor', axis=0, tiled=True...  43 us
    ppermute x2, waiting for transfers between devices, passed_along(): return lax.ppermute(shard, axis, pairs)  37.9 us
    psum x3, blocking collectives, body(): lax.psum(jnp.sum(apply_as_float * apply_as_float, axis=0), 'tensor')  32.6 us
    psum x1, blocking collectives, body(): lax.psum((jnp.stack(sum_rows) * live_section, jnp.stack(count_rows) * liv...  11.8 us
    psum x1, blocking collectives, body(): score_list.append(lax.psum(partial_score, 'tensor'))  9.71 us
    psum x1, blocking collectives, body(): squares = lax.psum(squares_part, 'tensor')  9.05 us
  transfers between devices with their start and end apart: 5, of which 5 were waited for; matrix products, arithmetic and copies ran while one was open for 0% of the time, Pallas kernels for 0%

commit v1 on v0

v1 whole, which is shorter than its diff:
```python
import functools

import jax
import jax.numpy as jnp
from jax import lax
from jax.experimental import pallas as pl
from jax.experimental.pallas import tpu as pltpu
from jax.sharding import PartitionSpec as P

SEGS = 16
LANES = 128
epsilon = 1e-05
MESH = pl.DeviceIdType.MESH


def each(low, high, step):
    if high - low <= 8:
        for i in range(low, high):
            step(i)
    else:
        lax.fori_loop(low, high, lambda i, _: (step(i), 0)[1], 0)


def row_tile(rows):
    return next(t for t in range(256, 0, -16) if rows % t == 0)


def kernel(
    tensor_n,
    dp_n,
    micros,
    width,
    rows,
    tok_ref,
    w_ref,
    cols_ref,
    labels_ref,
    mask_ref,
    seg_ref,
    out_ref,
    loss_ref,
    w,
    x,
    g,
    sq,
    o,
    parts,
    lc,
    w_sem,
    tok_sem,
    out_sem,
    g_send,
    g_recv,
    q_send,
    q_recv,
    x_send,
    x_recv,
    p_send,
    p_recv,
    l_send,
    l_recv,
):
    chunks = x.shape[0]
    per_micro = chunks // micros
    tile = row_tile(rows)
    tiles = rows // tile
    sec = lax.axis_index("section")
    dp = lax.axis_index("dp")
    me = lax.axis_index("tensor")
    group = 2 * dp_n
    place = sec * dp_n + dp

    def around(d):
        return lax.rem(me + d, tensor_n)

    def cousin(k):
        there = lax.rem(place + k, group)
        return {"section": there // dp_n, "dp": lax.rem(there, dp_n)}

    barrier = pltpu.get_barrier_semaphore()
    each(
        1,
        tensor_n,
        lambda d: pl.semaphore_signal(
            barrier, inc=1, device_id={"tensor": around(d)}, device_id_type=MESH
        ),
    )
    each(
        1,
        group,
        lambda k: pl.semaphore_signal(
            barrier, inc=1, device_id=cousin(k), device_id_type=MESH
        ),
    )

    load_w = pltpu.make_async_copy(w_ref, w, w_sem)

    def load_tok(c):
        return pltpu.make_async_copy(
            tok_ref.at[c // per_micro, :, pl.ds((c % per_micro) * LANES, LANES)],
            x.at[c],
            tok_sem.at[c],
        )

    def store_out(c):
        return pltpu.make_async_copy(
            o.at[c],
            out_ref.at[c // per_micro, :, pl.ds((c % per_micro) * LANES, LANES)],
            out_sem.at[c],
        )

    def block(c, owner):
        return g.at[c, pl.ds(pl.multiple_of(owner * rows, 16), rows), :]

    def gather_copy(c, owner, peer, d):
        return pltpu.make_async_remote_copy(
            src_ref=block(c, owner),
            dst_ref=block(c, owner),
            send_sem=g_send.at[c, d],
            recv_sem=g_recv.at[c, owner],
            device_id={"tensor": peer},
            device_id_type=MESH,
        )

    def square_copy(c, owner, peer, d):
        return pltpu.make_async_remote_copy(
            src_ref=sq.at[c, owner],
            dst_ref=sq.at[c, owner],
            send_sem=q_send.at[c, d],
            recv_sem=q_recv.at[c, owner],
            device_id={"tensor": peer},
            device_id_type=MESH,
        )

    def part_copy(c, owner, peer, d):
        return pltpu.make_async_remote_copy(
            src_ref=parts.at[c, owner],
            dst_ref=parts.at[c, owner],
            send_sem=p_send.at[c, d],
            recv_sem=p_recv.at[c, owner],
            device_id={"tensor": peer},
            device_id_type=MESH,
        )

    def handoff(c):
        return pltpu.make_async_remote_copy(
            src_ref=o.at[c],
            dst_ref=x.at[c],
            send_sem=x_send.at[c],
            recv_sem=x_recv.at[c],
            device_id={"section": 1 - sec},
            device_id_type=MESH,
        )

    def loss_copy(owner, k):
        return pltpu.make_async_remote_copy(
            src_ref=lc.at[owner],
            dst_ref=lc.at[owner],
            send_sem=l_send.at[k],
            recv_sem=l_recv.at[owner],
            device_id=cousin(k),
            device_id_type=MESH,
        )

    @pl.when(sec == 0)
    def _():
        for c in range(chunks):
            load_tok(c).start()

    load_w.start()
    pl.semaphore_wait(barrier, tensor_n - 1 + group - 1)

    def ready(c):
        @pl.when(sec == 0)
        def _():
            load_tok(c).wait()

        @pl.when(sec == 1)
        def _():
            handoff(c).wait_recv()

    def folded(v):
        return jnp.sum(v.reshape(v.shape[0] // 8, 8, LANES), axis=0)

    def prepare(c):
        def step(i, total):
            at = pl.multiple_of(i * tile, 16)
            v = x[c, pl.ds(at, tile), :].astype(jnp.float32)
            gain = cols_ref[pl.ds(at, tile), 0:1]
            g[c, pl.ds(pl.multiple_of(me * rows + at, 16), tile), :] = (v * gain).astype(
                jnp.bfloat16
            )
            return total + folded(v * v)

        sq[c, me] = lax.fori_loop(0, tiles, step, jnp.zeros((8, LANES), jnp.float32))

    def send(c):
        def one(d):
            square_copy(c, me, around(d), d).start()
            gather_copy(c, me, around(d), d).start()

        each(1, tensor_n, one)

    def sent(c):
        def one(d):
            square_copy(c, me, around(d), d).wait_send()
            gather_copy(c, me, around(d), d).wait_send()

        each(1, tensor_n, one)

    def arrived(c):
        def one(d):
            square_copy(c, around(d), around(d), d).wait_recv()
            gather_copy(c, around(d), around(d), d).wait_recv()

        each(1, tensor_n, one)

    def over_tensor(ref, c, low):
        total = ref[c, 0, low : low + 8, :]
        for t in range(1, tensor_n):
            total = total + ref[c, t, low : low + 8, :]
        return jnp.sum(total, axis=0, keepdims=True)

    def compute(c):
        q = lax.rsqrt(over_tensor(sq, c, 0) / width + epsilon)

        def step(i, totals):
            at = pl.multiple_of(i * tile, 16)
            mixed = q * jnp.dot(
                w[pl.ds(at, tile), :], g[c], preferred_element_type=jnp.float32
            )
            v = x[c, pl.ds(at, tile), :].astype(jnp.float32)
            result = (v + mixed / (1.0 + jnp.exp(-mixed))).astype(jnp.bfloat16)
            o[c, pl.ds(at, tile), :] = result
            f = result.astype(jnp.float32)
            head = cols_ref[pl.ds(at, tile), 1:2]
            return totals[0] + folded(f * f), totals[1] + folded(f * head)

        zero = jnp.zeros((8, LANES), jnp.float32)
        squares, dots = lax.fori_loop(0, tiles, step, (zero, zero))
        parts[c, me, 0:8, :] = squares
        parts[c, me, 8:16, :] = dots

    ready(0)
    prepare(0)
    send(0)
    for c in range(chunks):
        if c + 1 < chunks:
            ready(c + 1)
            prepare(c + 1)
        sent(c)
        if c + 1 < chunks:
            send(c + 1)
        arrived(c)
        if c == 0:
            load_w.wait()
        compute(c)
        store_out(c).start()

        @pl.when(sec == 0)
        def _():
            handoff(c).start()

        @pl.when(sec == 1)
        def _():
            each(1, tensor_n, lambda d: part_copy(c, me, around(d), d).start())

    @pl.when(sec == 1)
    def _():
        segment = lax.broadcasted_iota(jnp.int32, (SEGS, LANES), 0)
        for m in range(micros):
            losses = jnp.zeros((SEGS, LANES), jnp.float32)
            counts = jnp.zeros((SEGS, LANES), jnp.float32)
            for h in range(per_micro):
                c = m * per_micro + h
                each(
                    1,
                    tensor_n,
                    lambda d: part_copy(c, around(d), around(d), d).wait_recv(),
                )
                cut = slice(h * LANES, (h + 1) * LANES)
                inv_root = lax.rsqrt(over_tensor(parts, c, 0) / width + epsilon)
                scores = over_tensor(parts, c, 8) * inv_root
                weight = mask_ref[m : m + 1, cut].astype(jnp.float32)
                off = scores - (labels_ref[m : m + 1, cut].astype(jnp.float32) - 1.0)
                member = seg_ref[m : m + 1, cut] == segment
                losses += jnp.where(member, weight * off * off, 0.0)
                counts += jnp.where(member, weight, 0.0)
            lc[dp, m * SEGS : (m + 1) * SEGS, :] = losses
            lc[dp, (micros + m) * SEGS : (micros + m + 1) * SEGS, :] = counts
        each(1, group, lambda k: loss_copy(dp, k).start())
        each(1, dp_n, lambda k: loss_copy(lax.rem(dp + k, dp_n), k).wait_recv())

    @pl.when(sec == 0)
    def _():
        each(0, dp_n, lambda k: loss_copy(lax.rem(dp + k, dp_n), 1 + k).wait_recv())

    total = lc[0]
    for k in range(1, dp_n):
        total = total + lc[k]
    total = jnp.sum(total, axis=1, keepdims=True)
    half = micros * SEGS
    loss = total[:half] / jnp.maximum(total[half:], 1.0)
    loss_ref[...] = jnp.broadcast_to(loss, loss_ref.shape)

    for c in range(chunks):
        store_out(c).wait()

    @pl.when(sec == 0)
    def _():
        for c in range(chunks):
            handoff(c).wait_send()

    @pl.when(sec == 1)
    def _():
        for c in range(chunks):
            each(1, tensor_n, lambda d: part_copy(c, me, around(d), d).wait_send())
        each(1, group, lambda k: loss_copy(dp, k).wait_send())


def body(
    tensor_n,
    dp_n,
    tokens_in,
    section_proj,
    section_gain,
    final_gain,
    score_weight,
    labels,
    loss_mask,
    segment_ids,
):
    micros, rows, tokens = tokens_in.shape
    width = section_proj.shape[2]
    chunks = micros * (tokens // LANES)
    cols = jnp.stack(
        [
            section_gain[0].astype(jnp.float32),
            final_gain.astype(jnp.float32) * score_weight.astype(jnp.float32),
        ],
        axis=1,
    )
    dma = pltpu.SemaphoreType.DMA
    vmem = pl.BlockSpec(memory_space=pltpu.VMEM)
    hbm = pl.BlockSpec(memory_space=pl.ANY)
    out, loss = pl.pallas_call(
        functools.partial(kernel, tensor_n, dp_n, micros, width, rows),
        out_shape=(
            jax.ShapeDtypeStruct((micros, rows, tokens), jnp.bfloat16),
            jax.ShapeDtypeStruct((micros * SEGS, LANES), jnp.float32),
        ),
        in_specs=[hbm, hbm, vmem, vmem, vmem, vmem],
        out_specs=(hbm, vmem),
        scratch_shapes=[
            pltpu.VMEM((rows, width), jnp.bfloat16),
            pltpu.VMEM((chunks, rows, LANES), jnp.bfloat16),
            pltpu.VMEM((chunks, width, LANES), jnp.bfloat16),
            pltpu.VMEM((chunks, tensor_n, 8, LANES), jnp.float32),
            pltpu.VMEM((chunks, rows, LANES), jnp.bfloat16),
            pltpu.VMEM((chunks, tensor_n, 16, LANES), jnp.float32),
            pltpu.VMEM((dp_n, 2 * micros * SEGS, LANES), jnp.float32),
            dma,
            dma((chunks,)),
            dma((chunks,)),
            dma((chunks, tensor_n)),
            dma((chunks, tensor_n)),
            dma((chunks, tensor_n)),
            dma((chunks, tensor_n)),
            dma((chunks,)),
            dma((chunks,)),
            dma((chunks, tensor_n)),
            dma((chunks, tensor_n)),
            dma((2 * dp_n,)),
            dma((dp_n,)),
        ],
        compiler_params=pltpu.CompilerParams(
            collective_id=0, has_side_effects=True, vmem_limit_bytes=56 * 2**20
        ),
        cost_estimate=pl.CostEstimate(
            flops=2 * rows * width * micros * tokens,
            bytes_accessed=2 * rows * width,
            transcendentals=0,
        ),
        name="relay",
    )(tokens_in, section_proj[0], cols, labels, loss_mask, segment_ids)
    return out[None], loss[:, 0].reshape(micros, SEGS)


def solution(mesh):
    in_specs = (
        P(None, "tensor", "dp"),
        P("section", "tensor", None),
        P("section", "tensor"),
        P("tensor"),
        P("tensor"),
        P(None, "dp"),
        P(None, "dp"),
        P(None, "dp"),
    )
    out_specs = (P("section", None, "tensor", "dp"), P())
    return jax.shard_map(
        functools.partial(body, mesh.shape["tensor"], mesh.shape["dp"]),
        mesh=mesh,
        in_specs=in_specs,
        out_specs=out_specs,
        check_vma=False,
    )
```

time: 395 us -> 273 us (0.69)
  Pallas kernels: 0 us -> 265 us
  waiting for transfers between devices: 252 us -> 0 us
  blocking collectives: 63.2 us -> 0 us
  matrix products: 44 us -> 0 us
  between operations: 14 us -> 0.65 us
  starting transfers between devices: 7.99 us -> 0 us
  other arithmetic: 7.74 us -> 1.43 us
    pallas_call x0 -> x1, Pallas kernels: none -> 265 us  [body(): pl.pallas_call(functools.partial(kernel, tensor_n, dp_n, micros, width, r...]
    all_gather x3 -> x0, waiting for transfers between devices: 214 us -> none  [body(): lax.all_gather(normed, 'tensor', axis=0, tiled=True)]
    psum x6 -> x0, blocking collectives: 63.2 us -> none  [the longest x3 32.6 us: body(): lax.psum(jnp.sum(apply_as_float * apply_as_float, axis=0), 'tensor')]
    dot_general x7 -> x0, matrix products: 44 us -> none  [the longest x3 43 us: body(): jnp.dot(weight_local, lax.all_gather(normed, 'tensor', axis=0, tiled=True...]
    ppermute x2 -> x0, waiting for transfers between devices: 37.9 us -> none  [passed_along(): return lax.ppermute(shard, axis, pairs)]
    ppermute x2 -> x0, starting transfers between devices: 7.87 us -> none  [passed_along(): return lax.ppermute(shard, axis, pairs)]
  transfers between devices with their start and end apart: 5 -> 0, of which waited for: 5 -> 0; matrix products, arithmetic and copies ran while one was open for 0% -> 0% of each run, Pallas kernels for 0% -> 0%
where the time goes in v1:
time: 273 us; the launch traced here: 272 us
  Pallas kernels  265 us (97%)
  local copies, waits for them, and re-layouts  5.6 us (2%)
    pallas_call x1, Pallas kernels, body(): pl.pallas_call(functools.partial(kernel, tensor_n, dp_n, micros, width, r...  265 us

profile of v1, /device:TPU:0, one launch (start us, length us, event | category | flops | bytes accessed | tf_op | source)
XLA Modules:
  0.0 272.2 jit_solution(13183485896686510779)
XLA Ops:
  0.6 0.7 bitcast_convert_fusion
  1.3 0.7 convert_multiply_fusion
  2.1 1.3 copy.12.cols_ref
  3.3 264.5 %relay.1 = (bf16[2,1792,256]{2,1,0:T(8,128)(2,1)}, f32[32,128]{1,0:T(8,128)}) custom-call(bf16[2,1792,256]{2,1,0:T(8,128)(2,1)} %tok_ref.1, bf16[1792,7168]{1,0:T(8,128)(2,1)} %bitcast.6, f32[1792,2]{1,0:T(8,128)} %copy.12.cols_ref, s32[2,256]{1,0:T(2,128)} %labels_ref.1, s32[2,256]{1,0:T(2,128)} %mask_ref.1, s32[2,256]{1,0:T(2,128)} %seg_ref.1), custom_call_target="tpu_custom_call" | custom-call | flops 13153337344 | bytes 25690112 | tf_op jit(solution)/shard_map/relay/pallas_call | solution.py:346
  267.9 0.8 slice_reduce_fusion
  268.7 0.7 reshape_squeeze.3
  269.3 2.8 %copy.14 = bf16[1,2,1792,256]{3,2,1,0:T(8,128)(2,1)} copy(bf16[1,2,1792,256]{3,2,1,0:T(8,128)(2,1)} %bitcast.5) | data formatting | bytes 3670016
  (2 shorter events, 0.0 us)

commit v2 on v1

--- a/solution.py
+++ b/solution.py
@@ -44,6 +44,7 @@
     g,
     sq,
     o,
+    acc,
     parts,
     lc,
     w_sem,
@@ -64,6 +65,7 @@
     per_micro = chunks // micros
     tile = row_tile(rows)
     tiles = rows // tile
+    band_rows = rows // 2 if rows % 32 == 0 else rows
     sec = lax.axis_index("section")
     dp = lax.axis_index("dp")
     me = lax.axis_index("tensor")
@@ -208,12 +210,9 @@
 
         each(1, tensor_n, one)
 
-    def arrived(c):
-        def one(d):
-            square_copy(c, around(d), around(d), d).wait_recv()
-            gather_copy(c, around(d), around(d), d).wait_recv()
-
-        each(1, tensor_n, one)
+    def arrived(c, d):
+        square_copy(c, around(d), around(d), d).wait_recv()
+        gather_copy(c, around(d), around(d), d).wait_recv()
 
     def over_tensor(ref, c, low):
         total = ref[c, 0, low : low + 8, :]
@@ -221,14 +220,38 @@
             total = total + ref[c, t, low : low + 8, :]
         return jnp.sum(total, axis=0, keepdims=True)
 
-    def compute(c):
+    def multiply(c, owner, first):
+        at = pl.multiple_of(owner * rows, 16)
+        held = g[c, pl.ds(at, rows), :]
+
+        def step(i, _):
+            band = pl.ds(pl.multiple_of(i * band_rows, 16), band_rows)
+            product = jnp.dot(
+                w[band, pl.ds(pl.multiple_of(owner * rows, LANES), rows)],
+                held,
+                preferred_element_type=jnp.float32,
+            )
+            acc[band, :] = product if first else acc[band, :] + product
+            return 0
+
+        lax.fori_loop(0, rows // band_rows, step, 0)
+
+    def multiply_all(c):
+        def step(i, _):
+            band = pl.ds(pl.multiple_of(i * tile, 16), tile)
+            acc[band, :] = jnp.dot(
+                w[band, :], g[c], preferred_element_type=jnp.float32
+            )
+            return 0
+
+        lax.fori_loop(0, tiles, step, 0)
+
+    def finish(c):
         q = lax.rsqrt(over_tensor(sq, c, 0) / width + epsilon)
 
         def step(i, totals):
             at = pl.multiple_of(i * tile, 16)
-            mixed = q * jnp.dot(
-                w[pl.ds(at, tile), :], g[c], preferred_element_type=jnp.float32
-            )
+            mixed = q * acc[pl.ds(at, tile), :]
             v = x[c, pl.ds(at, tile), :].astype(jnp.float32)
             result = (v + mixed / (1.0 + jnp.exp(-mixed))).astype(jnp.bfloat16)
             o[c, pl.ds(at, tile), :] = result
@@ -240,6 +263,21 @@
         squares, dots = lax.fori_loop(0, tiles, step, (zero, zero))
         parts[c, me, 0:8, :] = squares
         parts[c, me, 8:16, :] = dots
+
+    def compute(c):
+        if rows % LANES:
+            each(1, tensor_n, lambda d: arrived(c, d))
+            multiply_all(c)
+        else:
+            multiply(c, me, True)
+
+            def one(d, _):
+                arrived(c, d)
+                multiply(c, around(d), False)
+                return 0
+
+            lax.fori_loop(1, tensor_n, one, 0)
+        finish(c)
 
     ready(0)
     prepare(0)
@@ -251,7 +289,6 @@
         sent(c)
         if c + 1 < chunks:
             send(c + 1)
-        arrived(c)
         if c == 0:
             load_w.wait()
         compute(c)
@@ -357,6 +394,7 @@
             pltpu.VMEM((chunks, width, LANES), jnp.bfloat16),
             pltpu.VMEM((chunks, tensor_n, 8, LANES), jnp.float32),
             pltpu.VMEM((chunks, rows, LANES), jnp.bfloat16),
+            pltpu.VMEM((rows, LANES), jnp.float32),
             pltpu.VMEM((chunks, tensor_n, 16, LANES), jnp.float32),
             pltpu.VMEM((dp_n, 2 * micros * SEGS, LANES), jnp.float32),
             dma,

time: 273 us -> 270 us (0.989)
  Pallas kernels: 265 us -> 262 us
where the time goes in v2:
time: 270 us
  Pallas kernels  262 us (97%)
  local copies, waits for them, and re-layouts  5.6 us (2%)
    pallas_call x1, Pallas kernels, body(): pl.pallas_call(functools.partial(kernel, tensor_n, dp_n, micros, width, r...  262 us

profile of v2, /device:TPU:0, one launch (start us, length us, event | category | flops | bytes accessed | tf_op | source)
XLA Modules:
  0.0 270.0 jit_solution(401855043681208613)
XLA Ops:
  0.6 0.7 bitcast_convert_fusion
  1.3 0.7 convert_multiply_fusion
  2.1 1.3 copy.12.cols_ref
  3.3 262.3 %relay.1 = (bf16[2,1792,256]{2,1,0:T(8,128)(2,1)}, f32[32,128]{1,0:T(8,128)}) custom-call(bf16[2,1792,256]{2,1,0:T(8,128)(2,1)} %tok_ref.1, bf16[1792,7168]{1,0:T(8,128)(2,1)} %bitcast.6, f32[1792,2]{1,0:T(8,128)} %copy.12.cols_ref, s32[2,256]{1,0:T(2,128)} %labels_ref.1, s32[2,256]{1,0:T(2,128)} %mask_ref.1, s32[2,256]{1,0:T(2,128)} %seg_ref.1), custom_call_target="tpu_custom_call" | custom-call | flops 13153337344 | bytes 25690112 | tf_op jit(solution)/shard_map/relay/pallas_call | solution.py:383
  265.7 0.8 slice_reduce_fusion
  266.5 0.7 reshape_squeeze.3
  267.1 2.8 %copy.14 = bf16[1,2,1792,256]{3,2,1,0:T(8,128)(2,1)} copy(bf16[1,2,1792,256]{3,2,1,0:T(8,128)(2,1)} %bitcast.5) | data formatting | bytes 3670016
  (2 shorter events, 0.0 us)

commit v3 on v2

--- a/solution.py
+++ b/solution.py
@@ -19,6 +19,10 @@
             step(i)
     else:
         lax.fori_loop(low, high, lambda i, _: (step(i), 0)[1], 0)
+
+
+def each_if(low, high, step):
+    lax.fori_loop(low, high, lambda i, _: (step(i), 0)[1], 0)
 
 
 def row_tile(rows):
@@ -114,13 +118,13 @@
     def block(c, owner):
         return g.at[c, pl.ds(pl.multiple_of(owner * rows, 16), rows), :]
 
-    def gather_copy(c, owner, peer, d):
+    def hop(c, owner, by, slot):
         return pltpu.make_async_remote_copy(
             src_ref=block(c, owner),
             dst_ref=block(c, owner),
-            send_sem=g_send.at[c, d],
+            send_sem=g_send.at[c, slot],
             recv_sem=g_recv.at[c, owner],
-            device_id={"tensor": peer},
+            device_id={"tensor": lax.rem(me + by + tensor_n, tensor_n)},
             device_id_type=MESH,
         )
 
@@ -196,23 +200,50 @@
 
         sq[c, me] = lax.fori_loop(0, tiles, step, jnp.zeros((8, LANES), jnp.float32))
 
+    has_right = me + 1 < tensor_n
+    has_left = me > 0
+
     def send(c):
-        def one(d):
-            square_copy(c, me, around(d), d).start()
-            gather_copy(c, me, around(d), d).start()
-
-        each(1, tensor_n, one)
+        each(1, tensor_n, lambda d: square_copy(c, me, around(d), d).start())
+
+        @pl.when(has_right)
+        def _():
+            hop(c, me, 1, me).start()
+
+        @pl.when(has_left)
+        def _():
+            hop(c, me, -1, tensor_n).start()
 
     def sent(c):
-        def one(d):
-            square_copy(c, me, around(d), d).wait_send()
-            gather_copy(c, me, around(d), d).wait_send()
-
-        each(1, tensor_n, one)
-
-    def arrived(c, d):
-        square_copy(c, around(d), around(d), d).wait_recv()
-        gather_copy(c, around(d), around(d), d).wait_recv()
+        each(1, tensor_n, lambda d: square_copy(c, me, around(d), d).wait_send())
+
+        @pl.when(has_right)
+        def _():
+            each_if(0, me + 1, lambda s: hop(c, s, 1, s).wait_send())
+
+        @pl.when(has_left)
+        def _():
+            hop(c, me, -1, tensor_n).wait_send()
+            each_if(me + 1, tensor_n, lambda s: hop(c, s, -1, s).wait_send())
+
+    def arrived(c, j):
+        @pl.when(me - j >= 0)
+        def _():
+            owner = me - j
+            hop(c, owner, 1, owner).wait_recv()
+
+            @pl.when(has_right)
+            def _():
+                hop(c, owner, 1, owner).start()
+
+        @pl.when(me + j < tensor_n)
+        def _():
+            owner = me + j
+            hop(c, owner, -1, owner).wait_recv()
+
+            @pl.when(has_left)
+            def _():
+                hop(c, owner, -1, owner).start()
 
     def over_tensor(ref, c, low):
         total = ref[c, 0, low : low + 8, :]
@@ -236,6 +267,15 @@
 
         lax.fori_loop(0, rows // band_rows, step, 0)
 
+    def both(c, j):
+        @pl.when(me - j >= 0)
+        def _():
+            multiply(c, me - j, False)
+
+        @pl.when(me + j < tensor_n)
+        def _():
+            multiply(c, me + j, False)
+
     def multiply_all(c):
         def step(i, _):
             band = pl.ds(pl.multiple_of(i * tile, 16), tile)
@@ -265,30 +305,33 @@
         parts[c, me, 8:16, :] = dots
 
     def compute(c):
-        if rows % LANES:
-            each(1, tensor_n, lambda d: arrived(c, d))
+        whole = rows % LANES != 0
+        if not whole:
+            multiply(c, me, True)
+
+        def step(j, _):
+            arrived(c, j)
+            if c + 1 < chunks:
+                @pl.when(j == max(1, tensor_n - 2))
+                def _():
+                    ready(c + 1)
+                    prepare(c + 1)
+                    send(c + 1)
+
+            if not whole:
+                both(c, j)
+            return 0
+
+        lax.fori_loop(1, tensor_n, step, 0)
+        if whole:
             multiply_all(c)
-        else:
-            multiply(c, me, True)
-
-            def one(d, _):
-                arrived(c, d)
-                multiply(c, around(d), False)
-                return 0
-
-            lax.fori_loop(1, tensor_n, one, 0)
+        each(1, tensor_n, lambda d: square_copy(c, around(d), around(d), d).wait_recv())
         finish(c)
 
     ready(0)
     prepare(0)
     send(0)
     for c in range(chunks):
-        if c + 1 < chunks:
-            ready(c + 1)
-            prepare(c + 1)
-        sent(c)
-        if c + 1 < chunks:
-            send(c + 1)
         if c == 0:
             load_w.wait()
         compute(c)
@@ -341,6 +384,7 @@
     loss_ref[...] = jnp.broadcast_to(loss, loss_ref.shape)
 
     for c in range(chunks):
+        sent(c)
         store_out(c).wait()
 
     @pl.when(sec == 0)
@@ -400,7 +444,7 @@
             dma,
             dma((chunks,)),
             dma((chunks,)),
-            dma((chunks, tensor_n)),
+            dma((chunks, tensor_n + 1)),
             dma((chunks, tensor_n)),
             dma((chunks, tensor_n)),
             dma((chunks, tensor_n)),

time: 270 us -> 191 us (0.71)
  Pallas kernels: 262 us -> 183 us
    pallas_call x1, Pallas kernels: 262 us -> 183 us  [body(): pl.pallas_call(functools.partial(kernel, tensor_n, dp_n, micros, width, r...]
where the time goes in v3:
time: 191 us; the launch traced here: 190 us
  Pallas kernels  183 us (96%)
  local copies, waits for them, and re-layouts  5.6 us (3%)
    pallas_call x1, Pallas kernels, body(): pl.pallas_call(functools.partial(kernel, tensor_n, dp_n, micros, width, r...  183 us

profile of v3, /device:TPU:0, one launch (start us, length us, event | category | flops | bytes accessed | tf_op | source)
XLA Modules:
  0.0 190.4 jit_solution(16176890946245742711)
XLA Ops:
  0.6 0.7 bitcast_convert_fusion
  1.3 0.7 convert_multiply_fusion
  2.1 1.3 copy.12.cols_ref
  3.3 182.7 %relay.1 = (bf16[2,1792,256]{2,1,0:T(8,128)(2,1)}, f32[32,128]{1,0:T(8,128)}) custom-call(bf16[2,1792,256]{2,1,0:T(8,128)(2,1)} %tok_ref.1, bf16[1792,7168]{1,0:T(8,128)(2,1)} %bitcast.6, f32[1792,2]{1,0:T(8,128)} %copy.12.cols_ref, s32[2,256]{1,0:T(2,128)} %labels_ref.1, s32[2,256]{1,0:T(2,128)} %mask_ref.1, s32[2,256]{1,0:T(2,128)} %seg_ref.1), custom_call_target="tpu_custom_call" | custom-call | flops 13153337344 | bytes 25690112 | tf_op jit(solution)/shard_map/relay/pallas_call | solution.py:427
  186.0 0.8 slice_reduce_fusion
  186.9 0.7 reshape_squeeze.3
  187.5 2.8 %copy.14 = bf16[1,2,1792,256]{3,2,1,0:T(8,128)(2,1)} copy(bf16[1,2,1792,256]{3,2,1,0:T(8,128)(2,1)} %bitcast.5) | data formatting | bytes 3670016
  (2 shorter events, 0.0 us)

commit v4 on v3

--- a/solution.py
+++ b/solution.py
@@ -49,6 +49,9 @@
     sq,
     o,
     acc,
+    own_gain,
+    other_gain,
+    relay,
     parts,
     lc,
     w_sem,
@@ -64,6 +67,11 @@
     p_recv,
     l_send,
     l_recv,
+    r_send,
+    r_recv,
+    c_send,
+    gain_send,
+    gain_recv,
 ):
     chunks = x.shape[0]
     per_micro = chunks // micros
@@ -101,12 +109,21 @@
 
     load_w = pltpu.make_async_copy(w_ref, w, w_sem)
 
-    def load_tok(c):
+    def load_tok(c, to):
         return pltpu.make_async_copy(
             tok_ref.at[c // per_micro, :, pl.ds((c % per_micro) * LANES, LANES)],
-            x.at[c],
+            to.at[c],
             tok_sem.at[c],
         )
+
+    gain_copy = pltpu.make_async_remote_copy(
+        src_ref=own_gain,
+        dst_ref=other_gain,
+        send_sem=gain_send,
+        recv_sem=gain_recv,
+        device_id={"section": 1 - sec},
+        device_id_type=MESH,
+    )
 
     def store_out(c):
         return pltpu.make_async_copy(
@@ -171,15 +188,29 @@
     @pl.when(sec == 0)
     def _():
         for c in range(chunks):
-            load_tok(c).start()
+            load_tok(c, x).start()
+
+    @pl.when(sec == 1)
+    def _():
+        load_tok(1, o).start()
 
     load_w.start()
+
+    def spread(i, _):
+        at = pl.ds(pl.multiple_of(i * tile, 16), tile)
+        own_gain[at, :] = jnp.broadcast_to(cols_ref[at, 0:1], (tile, LANES)).astype(
+            jnp.bfloat16
+        )
+        return 0
+
+    lax.fori_loop(0, tiles, spread, 0)
     pl.semaphore_wait(barrier, tensor_n - 1 + group - 1)
+    gain_copy.start()
 
     def ready(c):
         @pl.when(sec == 0)
         def _():
-            load_tok(c).wait()
+            load_tok(c, x).wait()
 
         @pl.when(sec == 1)
         def _():
@@ -203,47 +234,112 @@
     has_right = me + 1 < tensor_n
     has_left = me > 0
 
+    def lent(owner, by, slot):
+        at = relay.at[pl.ds(pl.multiple_of(owner * rows, 16), rows), :]
+        return pltpu.make_async_remote_copy(
+            src_ref=at,
+            dst_ref=at,
+            send_sem=r_send.at[slot],
+            recv_sem=r_recv.at[owner],
+            device_id={"tensor": lax.rem(me + by + tensor_n, tensor_n)},
+            device_id_type=MESH,
+        )
+
+    def cross(c, owner):
+        return pltpu.make_async_remote_copy(
+            src_ref=relay.at[pl.ds(pl.multiple_of(owner * rows, 16), rows), :],
+            dst_ref=block(c, owner),
+            send_sem=c_send.at[owner],
+            recv_sem=g_recv.at[c, owner],
+            device_id={"section": 1 - sec},
+            device_id_type=MESH,
+        )
+
+    def start_squares(c):
+        each(1, tensor_n, lambda d: square_copy(c, me, around(d), d).start())
+
+    def start_hops(copy):
+        @pl.when(has_right)
+        def _():
+            copy(me, 1, me).start()
+
+        @pl.when(has_left)
+        def _():
+            copy(me, -1, tensor_n).start()
+
+    def wait_hops(copy):
+        @pl.when(has_right)
+        def _():
+            each_if(0, me + 1, lambda s: copy(s, 1, s).wait_send())
+
+        @pl.when(has_left)
+        def _():
+            copy(me, -1, tensor_n).wait_send()
+            each_if(me + 1, tensor_n, lambda s: copy(s, -1, s).wait_send())
+
+    def hops(c):
+        return lambda owner, by, slot: hop(c, owner, by, slot)
+
     def send(c):
-        each(1, tensor_n, lambda d: square_copy(c, me, around(d), d).start())
-
-        @pl.when(has_right)
-        def _():
-            hop(c, me, 1, me).start()
-
-        @pl.when(has_left)
-        def _():
-            hop(c, me, -1, tensor_n).start()
-
-    def sent(c):
-        each(1, tensor_n, lambda d: square_copy(c, me, around(d), d).wait_send())
-
-        @pl.when(has_right)
-        def _():
-            each_if(0, me + 1, lambda s: hop(c, s, 1, s).wait_send())
-
-        @pl.when(has_left)
-        def _():
-            hop(c, me, -1, tensor_n).wait_send()
-            each_if(me + 1, tensor_n, lambda s: hop(c, s, -1, s).wait_send())
-
-    def arrived(c, j):
+        start_squares(c)
+        start_hops(hops(c))
+
+    def pass_on(copy, j, further=None):
         @pl.when(me - j >= 0)
         def _():
             owner = me - j
-            hop(c, owner, 1, owner).wait_recv()
+            copy(owner, 1, owner).wait_recv()
 
             @pl.when(has_right)
             def _():
-                hop(c, owner, 1, owner).start()
+                copy(owner, 1, owner).start()
+
+            if further:
+                further(owner)
 
         @pl.when(me + j < tensor_n)
         def _():
             owner = me + j
-            hop(c, owner, -1, owner).wait_recv()
+            copy(owner, -1, owner).wait_recv()
 
             @pl.when(has_left)
             def _():
-                hop(c, owner, -1, owner).start()
+                copy(owner, -1, owner).start()
+
+            if further:
+                further(owner)
+
+    def arrived(c, j):
+        pass_on(hops(c), j)
+
+    def crossed(c, j):
+        @pl.when(me - j >= 0)
+        def _():
+            cross(c, me - j).wait_recv()
+
+        @pl.when(me + j < tensor_n)
+        def _():
+            cross(c, me + j).wait_recv()
+
+    def lend(c):
+        gain_copy.wait_recv()
+
+        def step(i, _):
+            at = pl.multiple_of(i * tile, 16)
+            v = o[c, pl.ds(at, tile), :].astype(jnp.float32)
+            gain = other_gain[pl.ds(at, tile), :].astype(jnp.float32)
+            relay[pl.ds(pl.multiple_of(me * rows + at, 16), tile), :] = (v * gain).astype(
+                jnp.bfloat16
+            )
+            return 0
+
+        lax.fori_loop(0, tiles, step, 0)
+        start_hops(lent)
+        each_if(
+            1,
+            tensor_n,
+            lambda j: pass_on(lent, j, lambda owner: cross(c, owner).start()),
+        )
 
     def over_tensor(ref, c, low):
         total = ref[c, 0, low : low + 8, :]
@@ -304,20 +400,15 @@
         parts[c, me, 0:8, :] = squares
         parts[c, me, 8:16, :] = dots
 
-    def compute(c):
+    def run(c, meet, then=None, late=None):
         whole = rows % LANES != 0
         if not whole:
             multiply(c, me, True)
 
         def step(j, _):
-            arrived(c, j)
-            if c + 1 < chunks:
-                @pl.when(j == max(1, tensor_n - 2))
-                def _():
-                    ready(c + 1)
-                    prepare(c + 1)
-                    send(c + 1)
-
+            meet(j)
+            if then:
+                pl.when(j == max(1, tensor_n - 2))(then)
             if not whole:
                 both(c, j)
             return 0
@@ -325,25 +416,78 @@
         lax.fori_loop(1, tensor_n, step, 0)
         if whole:
             multiply_all(c)
+        if late:
+            late()
         each(1, tensor_n, lambda d: square_copy(c, around(d), around(d), d).wait_recv())
         finish(c)
-
-    ready(0)
-    prepare(0)
-    send(0)
-    for c in range(chunks):
-        if c == 0:
-            load_w.wait()
-        compute(c)
         store_out(c).start()
 
-        @pl.when(sec == 0)
-        def _():
-            handoff(c).start()
-
-        @pl.when(sec == 1)
-        def _():
+    assert chunks == 4
+    last = chunks - 1
+
+    @pl.when(sec == 0)
+    def _():
+        ready(0)
+        prepare(0)
+        send(0)
+        load_w.wait()
+
+        def then0():
+            ready(2)
+            prepare(2)
+            send(2)
+            ready(1)
+            prepare(1)
+            start_squares(1)
+
+        run(0, lambda j: arrived(0, j), then0)
+        handoff(0).start()
+
+        def meet1(j):
+            arrived(2, j)
+            crossed(1, j)
+
+        def then1():
+            ready(3)
+            prepare(3)
+            send(3)
+
+        run(1, meet1, then1)
+        handoff(1).start()
+        run(2, lambda j: None, None, lambda: arrived(3, 1))
+        handoff(2).start()
+        run(3, lambda j: pl.when(j > 1)(lambda: arrived(3, j)))
+        handoff(3).start()
+        lend(last)
+        for c in (0, 2, 3):
+            wait_hops(hops(c))
+
+    @pl.when(sec == 1)
+    def _():
+        load_tok(1, o).wait()
+        lend(1)
+        ready(0)
+        prepare(0)
+        send(0)
+        load_w.wait()
+        for c in range(chunks):
+
+            def then(c=c + 1):
+                ready(c)
+                prepare(c)
+                if c < last:
+                    send(c)
+                else:
+                    start_squares(c)
+
+            run(
+                c,
+                (lambda j: arrived(c, j)) if c < last else (lambda j: crossed(c, j)),
+                then if c < last else None,
+            )
             each(1, tensor_n, lambda d: part_copy(c, me, around(d), d).start())
+        for c in (0, 1, 2):
+            wait_hops(hops(c))
 
     @pl.when(sec == 1)
     def _():
@@ -384,8 +528,11 @@
     loss_ref[...] = jnp.broadcast_to(loss, loss_ref.shape)
 
     for c in range(chunks):
-        sent(c)
+        each(1, tensor_n, lambda d: square_copy(c, me, around(d), d).wait_send())
         store_out(c).wait()
+    wait_hops(lent)
+    each(1, tensor_n, lambda d: cross(1, around(d)).wait_send())
+    gain_copy.wait_send()
 
     @pl.when(sec == 0)
     def _():
@@ -439,6 +586,9 @@
             pltpu.VMEM((chunks, tensor_n, 8, LANES), jnp.float32),
             pltpu.VMEM((chunks, rows, LANES), jnp.bfloat16),
             pltpu.VMEM((rows, LANES), jnp.float32),
+            pltpu.VMEM((rows, LANES), jnp.bfloat16),
+            pltpu.VMEM((rows, LANES), jnp.bfloat16),
+            pltpu.VMEM((width, LANES), jnp.bfloat16),
             pltpu.VMEM((chunks, tensor_n, 16, LANES), jnp.float32),
             pltpu.VMEM((dp_n, 2 * micros * SEGS, LANES), jnp.float32),
             dma,
@@ -454,6 +604,11 @@
             dma((chunks, tensor_n)),
             dma((2 * dp_n,)),
             dma((dp_n,)),
+            dma((tensor_n + 1,)),
+            dma((tensor_n,)),
+            dma((tensor_n,)),
+            dma,
+            dma,
         ],
         compiler_params=pltpu.CompilerParams(
             collective_id=0, has_side_effects=True, vmem_limit_bytes=56 * 2**20

time: 191 us -> 168 us (0.88)
  Pallas kernels: 183 us -> 160 us
    pallas_call x1, Pallas kernels: 183 us -> 160 us  [body(): pl.pallas_call(functools.partial(kernel, tensor_n, dp_n, micros, width, r...]
where the time goes in v4:
time: 168 us
  Pallas kernels  160 us (95%)
  local copies, waits for them, and re-layouts  5.6 us (3%)
    pallas_call x1, Pallas kernels, body(): pl.pallas_call(functools.partial(kernel, tensor_n, dp_n, micros, width, r...  160 us

profile of v4, /device:TPU:0, one launch (start us, length us, event | category | flops | bytes accessed | tf_op | source)
XLA Modules:
  0.0 168.0 jit_solution(5036401685693060695)
XLA Ops:
  0.6 0.7 bitcast_convert_fusion
  1.3 0.7 convert_multiply_fusion
  2.1 1.3 copy.12.cols_ref
  3.3 160.4 %relay.1 = (bf16[2,1792,256]{2,1,0:T(8,128)(2,1)}, f32[32,128]{1,0:T(8,128)}) custom-call(bf16[2,1792,256]{2,1,0:T(8,128)(2,1)} %tok_ref.1, bf16[1792,7168]{1,0:T(8,128)(2,1)} %bitcast.6, f32[1792,2]{1,0:T(8,128)} %copy.12.cols_ref, s32[2,256]{1,0:T(2,128)} %labels_ref.1, s32[2,256]{1,0:T(2,128)} %mask_ref.1, s32[2,256]{1,0:T(2,128)} %seg_ref.1), custom_call_target="tpu_custom_call" | custom-call | flops 13153337344 | bytes 25690112 | tf_op jit(solution)/shard_map/relay/pallas_call | solution.py:574
  163.7 0.8 slice_reduce_fusion
  164.5 0.7 reshape_squeeze.3
  165.2 2.8 %copy.14 = bf16[1,2,1792,256]{3,2,1,0:T(8,128)(2,1)} copy(bf16[1,2,1792,256]{3,2,1,0:T(8,128)(2,1)} %bitcast.5) | data formatting | bytes 3670016
  (2 shorter events, 0.0 us)

commit v5 on v4

--- a/solution.py
+++ b/solution.py
@@ -165,12 +165,13 @@
             device_id_type=MESH,
         )
 
-    def handoff(c):
+    def handoff(c, i):
+        band = pl.ds(pl.multiple_of(i * tile, 16), tile)
         return pltpu.make_async_remote_copy(
-            src_ref=o.at[c],
-            dst_ref=x.at[c],
-            send_sem=x_send.at[c],
-            recv_sem=x_recv.at[c],
+            src_ref=o.at[c, band, :],
+            dst_ref=x.at[c, band, :],
+            send_sem=x_send.at[c, i],
+            recv_sem=x_recv.at[c, i],
             device_id={"section": 1 - sec},
             device_id_type=MESH,
         )
@@ -207,20 +208,16 @@
     pl.semaphore_wait(barrier, tensor_n - 1 + group - 1)
     gain_copy.start()
 
-    def ready(c):
-        @pl.when(sec == 0)
-        def _():
-            load_tok(c, x).wait()
-
-        @pl.when(sec == 1)
-        def _():
-            handoff(c).wait_recv()
-
     def folded(v):
         return jnp.sum(v.reshape(v.shape[0] // 8, 8, LANES), axis=0)
 
-    def prepare(c):
+    def prepare(c, handed):
+        if not handed:
+            load_tok(c, x).wait()
+
         def step(i, total):
+            if handed:
+                handoff(c, i).wait_recv()
             at = pl.multiple_of(i * tile, 16)
             v = x[c, pl.ds(at, tile), :].astype(jnp.float32)
             gain = cols_ref[pl.ds(at, tile), 0:1]
@@ -358,7 +355,7 @@
                 held,
                 preferred_element_type=jnp.float32,
             )
-            acc[band, :] = product if first else acc[band, :] + product
+            acc[c % 2, band, :] = product if first else acc[c % 2, band, :] + product
             return 0
 
         lax.fori_loop(0, rows // band_rows, step, 0)
@@ -375,22 +372,25 @@
     def multiply_all(c):
         def step(i, _):
             band = pl.ds(pl.multiple_of(i * tile, 16), tile)
-            acc[band, :] = jnp.dot(
+            acc[c % 2, band, :] = jnp.dot(
                 w[band, :], g[c], preferred_element_type=jnp.float32
             )
             return 0
 
         lax.fori_loop(0, tiles, step, 0)
 
-    def finish(c):
+    def finish(c, hand):
+        each(1, tensor_n, lambda d: square_copy(c, around(d), around(d), d).wait_recv())
         q = lax.rsqrt(over_tensor(sq, c, 0) / width + epsilon)
 
         def step(i, totals):
             at = pl.multiple_of(i * tile, 16)
-            mixed = q * acc[pl.ds(at, tile), :]
+            mixed = q * acc[c % 2, pl.ds(at, tile), :]
             v = x[c, pl.ds(at, tile), :].astype(jnp.float32)
             result = (v + mixed / (1.0 + jnp.exp(-mixed))).astype(jnp.bfloat16)
             o[c, pl.ds(at, tile), :] = result
+            if hand:
+                handoff(c, i).start()
             f = result.astype(jnp.float32)
             head = cols_ref[pl.ds(at, tile), 1:2]
             return totals[0] + folded(f * f), totals[1] + folded(f * head)
@@ -399,65 +399,69 @@
         squares, dots = lax.fori_loop(0, tiles, step, (zero, zero))
         parts[c, me, 0:8, :] = squares
         parts[c, me, 8:16, :] = dots
-
-    def run(c, meet, then=None, late=None):
-        whole = rows % LANES != 0
+        store_out(c).start()
+        if not hand:
+            each(1, tensor_n, lambda d: part_copy(c, me, around(d), d).start())
+
+    whole = rows % LANES != 0
+
+    def begin(c):
         if not whole:
             multiply(c, me, True)
+
+    def add(c, j):
+        if not whole:
+            both(c, j)
+
+    def close(c, hand):
+        if whole:
+            multiply_all(c)
+        finish(c, hand)
+
+    turn = max(1, tensor_n - 2)
+
+    def run(c, hand, meet, then=None):
+        begin(c)
 
         def step(j, _):
             meet(j)
             if then:
-                pl.when(j == max(1, tensor_n - 2))(then)
-            if not whole:
-                both(c, j)
+                pl.when(j == turn)(then)
+            add(c, j)
             return 0
 
         lax.fori_loop(1, tensor_n, step, 0)
-        if whole:
-            multiply_all(c)
-        if late:
-            late()
-        each(1, tensor_n, lambda d: square_copy(c, around(d), around(d), d).wait_recv())
-        finish(c)
-        store_out(c).start()
+        close(c, hand)
 
     assert chunks == 4
     last = chunks - 1
 
     @pl.when(sec == 0)
     def _():
-        ready(0)
-        prepare(0)
+        prepare(0, False)
         send(0)
         load_w.wait()
 
         def then0():
-            ready(2)
-            prepare(2)
+            prepare(2, False)
             send(2)
-            ready(1)
-            prepare(1)
+            prepare(1, False)
             start_squares(1)
 
-        run(0, lambda j: arrived(0, j), then0)
-        handoff(0).start()
+        run(0, True, lambda j: arrived(0, j), then0)
 
         def meet1(j):
-            arrived(2, j)
+            pl.when(j == 1)(lambda: arrived(2, 1))
             crossed(1, j)
 
-        def then1():
-            ready(3)
-            prepare(3)
+        run(1, True, meet1)
+
+        def then2():
+            prepare(3, False)
             send(3)
 
-        run(1, meet1, then1)
-        handoff(1).start()
-        run(2, lambda j: None, None, lambda: arrived(3, 1))
-        handoff(2).start()
-        run(3, lambda j: pl.when(j > 1)(lambda: arrived(3, j)))
-        handoff(3).start()
+        run(2, True, lambda j: pl.when(j > 1)(lambda: arrived(2, j)), then2)
+        run(3, True, lambda j: arrived(3, j))
         lend(last)
         for c in (0, 2, 3):
             wait_hops(hops(c))
@@ -466,26 +470,46 @@
     def _():
         load_tok(1, o).wait()
         lend(1)
-        ready(0)
-        prepare(0)
+        prepare(0, True)
         send(0)
         load_w.wait()
-        for c in range(chunks):
+        for c in range(last - 1):
 
             def then(c=c + 1):
-                ready(c)
-                prepare(c)
-                if c < last:
-                    send(c)
-                else:
-                    start_squares(c)
-
-            run(
-                c,
-                (lambda j: arrived(c, j)) if c < last else (lambda j: crossed(c, j)),
-                then if c < last else None,
-            )
-            each(1, tensor_n, lambda d: part_copy(c, me, around(d), d).start())
+                prepare(c, True)
+                send(c)
+
+            run(c, False, lambda j: arrived(c, j), then)
+
+        c = last - 1
+        begin(c)
+
+        def step(j, _):
+            arrived(c, j)
+            add(c, j)
+
+            @pl.when(j == turn)
+            def _():
+                prepare(last, True)
+                start_squares(last)
+                begin(last)
+
+            @pl.when(j > turn)
+            def _():
+                def catch_up(k, _):
+                    crossed(last, k)
+                    add(last, k)
+                    return 0
+
+                lax.fori_loop(1, turn + 1, catch_up, 0)
+
+            return 0
+
+        lax.fori_loop(1, tensor_n, step, 0)
+        close(c, False)
+        crossed(last, tensor_n - 1)
+        add(last, tensor_n - 1)
+        close(last, False)
         for c in (0, 1, 2):
             wait_hops(hops(c))
 
@@ -525,7 +549,12 @@
     total = jnp.sum(total, axis=1, keepdims=True)
     half = micros * SEGS
     loss = total[:half] / jnp.maximum(total[half:], 1.0)
-    loss_ref[...] = jnp.broadcast_to(loss, loss_ref.shape)
+    lane = lax.broadcasted_iota(jnp.int32, (SEGS, LANES), 1)
+    diagonal = lane == lax.broadcasted_iota(jnp.int32, (SEGS, LANES), 0)
+    for m in range(micros):
+        column = jnp.broadcast_to(loss[m * SEGS : (m + 1) * SEGS], (SEGS, LANES))
+        row = jnp.sum(jnp.where(diagonal, column, 0.0), axis=0, keepdims=True)
+        loss_ref[m : m + 1, :] = row[:, :SEGS]
 
     for c in range(chunks):
         each(1, tensor_n, lambda d: square_copy(c, me, around(d), d).wait_send())
@@ -537,7 +566,7 @@
     @pl.when(sec == 0)
     def _():
         for c in range(chunks):
-            handoff(c).wait_send()
+            each(0, tiles, lambda i: handoff(c, i).wait_send())
 
     @pl.when(sec == 1)
     def _():
@@ -575,7 +604,7 @@
         functools.partial(kernel, tensor_n, dp_n, micros, width, rows),
         out_shape=(
             jax.ShapeDtypeStruct((micros, rows, tokens), jnp.bfloat16),
-            jax.ShapeDtypeStruct((micros * SEGS, LANES), jnp.float32),
+            jax.ShapeDtypeStruct((micros, SEGS), jnp.float32),
         ),
         in_specs=[hbm, hbm, vmem, vmem, vmem, vmem],
         out_specs=(hbm, vmem),
@@ -585,7 +614,7 @@
             pltpu.VMEM((chunks, width, LANES), jnp.bfloat16),
             pltpu.VMEM((chunks, tensor_n, 8, LANES), jnp.float32),
             pltpu.VMEM((chunks, rows, LANES), jnp.bfloat16),
-            pltpu.VMEM((rows, LANES), jnp.float32),
+            pltpu.VMEM((2, rows, LANES), jnp.float32),
             pltpu.VMEM((rows, LANES), jnp.bfloat16),
             pltpu.VMEM((rows, LANES), jnp.bfloat16),
             pltpu.VMEM((width, LANES), jnp.bfloat16),
@@ -598,8 +627,8 @@
             dma((chunks, tensor_n)),
             dma((chunks, tensor_n)),
             dma((chunks, tensor_n)),
-            dma((chunks,)),
-            dma((chunks,)),
+            dma((chunks, rows // row_tile(rows))),
+            dma((chunks, rows // row_tile(rows))),
             dma((chunks, tensor_n)),
             dma((chunks, tensor_n)),
             dma((2 * dp_n,)),
@@ -620,7 +649,7 @@
         ),
         name="relay",
     )(tokens_in, section_proj[0], cols, labels, loss_mask, segment_ids)
-    return out[None], loss[:, 0].reshape(micros, SEGS)
+    return out[None], loss
 
 
 def solution(mesh):

time: 168 us -> 168 us (level)
    unnamed x1 -> x4, local copies, waits for them, and re-layouts: 2.84 us -> 3.41 us
where the time goes in v5:
time: 168 us
  Pallas kernels  161 us (96%)
  local copies, waits for them, and re-layouts  4.68 us (3%)
    pallas_call x1, Pallas kernels, body(): pl.pallas_call(functools.partial(kernel, tensor_n, dp_n, micros, width, r...  161 us
    unnamed x4, local copies, waits for them, and re-layouts  3.41 us

profile of v5, /device:TPU:0, one launch (start us, length us, event | category | flops | bytes accessed | tf_op | source)
XLA Modules:
  0.0 168.0 jit_solution(2970061502782971879)
XLA Ops:
  0.6 0.7 bitcast_convert_fusion
  1.3 0.7 convert_multiply_fusion
  2.1 1.3 copy.12.cols_ref
  3.3 161.3 %relay.1 = (bf16[2,1792,256]{2,1,0:T(8,128)(2,1)}, f32[2,16]{1,0:T(2,128)}) custom-call(bf16[2,1792,256]{2,1,0:T(8,128)(2,1)} %tok_ref.1, bf16[1792,7168]{1,0:T(8,128)(2,1)} %bitcast.6, f32[1792,2]{1,0:T(8,128)} %copy.12.cols_ref, s32[2,256]{1,0:T(2,128)} %labels_ref.1, s32[2,256]{1,0:T(2,128)} %mask_ref.1, s32[2,256]{1,0:T(2,128)} %seg_ref.1), custom_call_target="tpu_custom_call" | custom-call | flops 13153337344 | bytes 25690112 | tf_op jit(solution)/shard_map/relay/pallas_call | solution.py:603
  164.6 0.0 copy-start
  164.6 2.8 %copy.15 = bf16[1,2,1792,256]{3,2,1,0:T(8,128)(2,1)} copy(bf16[1,2,1792,256]{3,2,1,0:T(8,128)(2,1)} %bitcast.5) | data formatting | bytes 3670016
  167.5 0.0 copy-done
  167.5 0.6 copy.16
  (2 shorter events, 0.0 us)
Async XLA Ops:
  164.6 2.9 %copy-start = (f32[2,16]{1,0:T(2,128)S(1)}, f32[2,16]{1,0:T(2,128)}, u32[]{:S(2)}) copy-start(f32[2,16]{1,0:T(2,128)} %get-tuple-element.9) | copy-start | bytes 388

commit v6 on v5

--- a/solution.py
+++ b/solution.py
@@ -8,6 +8,7 @@
 from jax.sharding import PartitionSpec as P
 
 SEGS = 16
+PIECES = 2
 LANES = 128
 epsilon = 1e-05
 MESH = pl.DeviceIdType.MESH
@@ -132,15 +133,19 @@
             out_sem.at[c],
         )
 
-    def block(c, owner):
-        return g.at[c, pl.ds(pl.multiple_of(owner * rows, 16), rows), :]
-
-    def hop(c, owner, by, slot):
+    def piece_of(owner, h):
+        size = rows // PIECES
+        return pl.ds(pl.multiple_of(owner * rows + h * size, 16), size)
+
+    def block(c, owner, h):
+        return g.at[c, piece_of(owner, h), :]
+
+    def hop(c, owner, by, slot, h):
         return pltpu.make_async_remote_copy(
-            src_ref=block(c, owner),
-            dst_ref=block(c, owner),
-            send_sem=g_send.at[c, slot],
-            recv_sem=g_recv.at[c, owner],
+            src_ref=block(c, owner, h),
+            dst_ref=block(c, owner, h),
+            send_sem=g_send.at[c, slot, h],
+            recv_sem=g_recv.at[c, owner, h],
             device_id={"tensor": lax.rem(me + by + tensor_n, tensor_n)},
             device_id_type=MESH,
         )
@@ -231,23 +236,23 @@
     has_right = me + 1 < tensor_n
     has_left = me > 0
 
-    def lent(owner, by, slot):
-        at = relay.at[pl.ds(pl.multiple_of(owner * rows, 16), rows), :]
+    def lent(owner, by, slot, h):
+        at = relay.at[piece_of(owner, h), :]
         return pltpu.make_async_remote_copy(
             src_ref=at,
             dst_ref=at,
-            send_sem=r_send.at[slot],
-            recv_sem=r_recv.at[owner],
+            send_sem=r_send.at[slot, h],
+            recv_sem=r_recv.at[owner, h],
             device_id={"tensor": lax.rem(me + by + tensor_n, tensor_n)},
             device_id_type=MESH,
         )
 
-    def cross(c, owner):
+    def cross(c, owner, h):
         return pltpu.make_async_remote_copy(
-            src_ref=relay.at[pl.ds(pl.multiple_of(owner * rows, 16), rows), :],
-            dst_ref=block(c, owner),
-            send_sem=c_send.at[owner],
-            recv_sem=g_recv.at[c, owner],
+            src_ref=relay.at[piece_of(owner, h), :],
+            dst_ref=block(c, owner, h),
+            send_sem=c_send.at[owner, h],
+            recv_sem=g_recv.at[c, owner, h],
             device_id={"section": 1 - sec},
             device_id_type=MESH,
         )
@@ -256,67 +261,75 @@
         each(1, tensor_n, lambda d: square_copy(c, me, around(d), d).start())
 
     def start_hops(copy):
-        @pl.when(has_right)
-        def _():
-            copy(me, 1, me).start()
-
-        @pl.when(has_left)
-        def _():
-            copy(me, -1, tensor_n).start()
+        for h in range(PIECES):
+
+            @pl.when(has_right)
+            def _():
+                copy(me, 1, me, h).start()
+
+            @pl.when(has_left)
+            def _():
+                copy(me, -1, tensor_n, h).start()
 
     def wait_hops(copy):
-        @pl.when(has_right)
-        def _():
-            each_if(0, me + 1, lambda s: copy(s, 1, s).wait_send())
-
-        @pl.when(has_left)
-        def _():
-            copy(me, -1, tensor_n).wait_send()
-            each_if(me + 1, tensor_n, lambda s: copy(s, -1, s).wait_send())
+        for h in range(PIECES):
+
+            @pl.when(has_right)
+            def _():
+                each_if(0, me + 1, lambda s: copy(s, 1, s, h).wait_send())
+
+            @pl.when(has_left)
+            def _():
+                copy(me, -1, tensor_n, h).wait_send()
+                each_if(me + 1, tensor_n, lambda s: copy(s, -1, s, h).wait_send())
 
     def hops(c):
-        return lambda owner, by, slot: hop(c, owner, by, slot)
+        return lambda owner, by, slot, h: hop(c, owner, by, slot, h)
 
     def send(c):
         start_squares(c)
         start_hops(hops(c))
 
     def pass_on(copy, j, further=None):
-        @pl.when(me - j >= 0)
-        def _():
-            owner = me - j
-            copy(owner, 1, owner).wait_recv()
-
-            @pl.when(has_right)
-            def _():
-                copy(owner, 1, owner).start()
-
-            if further:
-                further(owner)
-
-        @pl.when(me + j < tensor_n)
-        def _():
-            owner = me + j
-            copy(owner, -1, owner).wait_recv()
-
-            @pl.when(has_left)
-            def _():
-                copy(owner, -1, owner).start()
-
-            if further:
-                further(owner)
+        for h in range(PIECES):
+
+            @pl.when(me - j >= 0)
+            def _():
+                owner = me - j
+                copy(owner, 1, owner, h).wait_recv()
+
+                @pl.when(has_right)
+                def _():
+                    copy(owner, 1, owner, h).start()
+
+                if further:
+                    further(owner, h)
+
+            @pl.when(me + j < tensor_n)
+            def _():
+                owner = me + j
+                copy(owner, -1, owner, h).wait_recv()
+
+                @pl.when(has_left)
+                def _():
+                    copy(owner, -1, owner, h).start()
+
+                if further:
+                    further(owner, h)
 
     def arrived(c, j):
         pass_on(hops(c), j)
 
     def crossed(c, j):
-        @pl.when(me - j >= 0)
-        def _():
-            cross(c, me - j).wait_recv()
-
-        @pl.when(me + j < tensor_n)
-        def _():
-            cross(c, me + j).wait_recv()
+        for h in range(PIECES):
+
+            @pl.when(me - j >= 0)
+            def _():
+                cross(c, me - j, h).wait_recv()
+
+            @pl.when(me + j < tensor_n)
+            def _():
+                cross(c, me + j, h).wait_recv()
 
     def lend(c):
         gain_copy.wait_recv()
@@ -335,7 +348,7 @@
         each_if(
             1,
             tensor_n,
-            lambda j: pass_on(lent, j, lambda owner: cross(c, owner).start()),
+            lambda j: pass_on(lent, j, lambda owner, h: cross(c, owner, h).start()),
         )
 
     def over_tensor(ref, c, low):
@@ -560,7 +573,8 @@
         each(1, tensor_n, lambda d: square_copy(c, me, around(d), d).wait_send())
         store_out(c).wait()
     wait_hops(lent)
-    each(1, tensor_n, lambda d: cross(1, around(d)).wait_send())
+    for h in range(PIECES):
+        each(1, tensor_n, lambda d: cross(1, around(d), h).wait_send())
     gain_copy.wait_send()
 
     @pl.when(sec == 0)
@@ -623,8 +637,8 @@
             dma,
             dma((chunks,)),
             dma((chunks,)),
-            dma((chunks, tensor_n + 1)),
-            dma((chunks, tensor_n)),
+            dma((chunks, tensor_n + 1, PIECES)),
+            dma((chunks, tensor_n, PIECES)),
             dma((chunks, tensor_n)),
             dma((chunks, tensor_n)),
             dma((chunks, rows // row_tile(rows))),
@@ -633,9 +647,9 @@
             dma((chunks, tensor_n)),
             dma((2 * dp_n,)),
             dma((dp_n,)),
-            dma((tensor_n + 1,)),
-            dma((tensor_n,)),
-            dma((tensor_n,)),
+            dma((tensor_n + 1, PIECES)),
+            dma((tensor_n, PIECES)),
+            dma((tensor_n, PIECES)),
             dma,
             dma,
         ],

time: 168 us -> 166 us (0.988)
  Pallas kernels: 161 us -> 159 us
    pallas_call x1, Pallas kernels: 161 us -> 159 us  [body(): pl.pallas_call(functools.partial(kernel, tensor_n, dp_n, micros, width, r...]
where the time goes in v6:
time: 166 us
  Pallas kernels  159 us (96%)
  local copies, waits for them, and re-layouts  4.68 us (3%)
    pallas_call x1, Pallas kernels, body(): pl.pallas_call(functools.partial(kernel, tensor_n, dp_n, micros, width, r...  159 us
    unnamed x4, local copies, waits for them, and re-layouts  3.41 us

profile of v6, /device:TPU:0, one launch (start us, length us, event | category | flops | bytes accessed | tf_op | source)
XLA Modules:
  0.0 166.1 jit_solution(9261758709367787681)
XLA Ops:
  0.6 0.7 bitcast_convert_fusion
  1.3 0.7 convert_multiply_fusion
  2.1 1.3 copy.12.cols_ref
  3.3 159.3 %relay.1 = (bf16[2,1792,256]{2,1,0:T(8,128)(2,1)}, f32[2,16]{1,0:T(2,128)}) custom-call(bf16[2,1792,256]{2,1,0:T(8,128)(2,1)} %tok_ref.1, bf16[1792,7168]{1,0:T(8,128)(2,1)} %bitcast.6, f32[1792,2]{1,0:T(8,128)} %copy.12.cols_ref, s32[2,256]{1,0:T(2,128)} %labels_ref.1, s32[2,256]{1,0:T(2,128)} %mask_ref.1, s32[2,256]{1,0:T(2,128)} %seg_ref.1), custom_call_target="tpu_custom_call" | custom-call | flops 13153337344 | bytes 25690112 | tf_op jit(solution)/shard_map/relay/pallas_call | solution.py:617
  162.7 0.0 copy-start
  162.7 2.8 %copy.15 = bf16[1,2,1792,256]{3,2,1,0:T(8,128)(2,1)} copy(bf16[1,2,1792,256]{3,2,1,0:T(8,128)(2,1)} %bitcast.5) | data formatting | bytes 3670016
  165.5 0.0 copy-done
  165.5 0.6 copy.16
  (2 shorter events, 0.0 us)
Async XLA Ops:
  162.7 2.9 %copy-start = (f32[2,16]{1,0:T(2,128)S(1)}, f32[2,16]{1,0:T(2,128)}, u32[]{:S(2)}) copy-start(f32[2,16]{1,0:T(2,128)} %get-tuple-element.9) | copy-start | bytes 388
